TPU v7x, 32 devices: a whole 2x2x4 slice. The times are simulated.
32 devices in a mesh: groups: 2 (over x), rows: 16 (over z, y, core).
Axes of the slice: x: 2, y: 2, z: 4, core: 2. Of those that a mesh axis runs over, the one named last changes fastest.
Arguments:
- pair: bfloat16 [512, 256, 128], P(('groups', 'rows')), parts along dimension 0, may hold values from -6 to 6
- proj_weights: bfloat16 [6, 128, 128], replicated, may hold values from -0.5 to 0.5
- cotangent: bfloat16 [512, 256, 128], P(('groups', 'rows')), parts along dimension 0, may hold values from -8.5 to 8.5
Outputs:
- update: bfloat16 [512, 256, 128], P(('groups', 'rows')), parts along dimension 0
- pair_grad: bfloat16 [512, 256, 128], P(('groups', 'rows')), parts along dimension 0
- weight_grads: float32 [12, 128, 128], P('groups'), parts along dimension 0
There are 2 independent parts, one for each index of `groups`. A program takes and returns all parts, laid end to end along the dimension named above; an argument that names none is the same for every part. Nothing has to cross between parts.
All inputs are finite; a program needn't handle non-finite values.
Results may differ from a plain program's by a relative error of at most 0.015.
Values may be sent and summed in bfloat16 or wider, within the bound.
A program may use at most 128 MiB of HBM per device.

v0:
```python
import jax
import jax.numpy as jnp
from jax import lax
from jax.sharding import PartitionSpec as P


def layer_norm(values, along_dim):
    centred = values - jnp.mean(values, axis=along_dim, keepdims=True)
    inv_scale = lax.rsqrt(jnp.mean(centred * centred, axis=along_dim, keepdims=True) + 1e-05)
    return (centred * inv_scale, inv_scale)


def norm_backward(normed, inv_scale, upstream, along_dim):
    return (
        upstream
        - jnp.mean(upstream, axis=along_dim, keepdims=True)
        - normed * jnp.mean(upstream * normed, axis=along_dim, keepdims=True)
    ) * inv_scale


def triangle_slab(pieces):
    left_slab, right_slab = pieces
    product = lax.dot_general(
        left_slab, right_slab, (((3,), (3,)), ((0, 1), (0, 1))), preferred_element_type=jnp.float32
    )
    return (product.astype(jnp.bfloat16), left_slab, right_slab)


def edge_backward(upstream, left_slab, right_slab):
    left_part = lax.dot_general(
        upstream, right_slab, (((3,), (2,)), ((0, 1), (0, 1))), preferred_element_type=jnp.float32
    )
    right_part = lax.dot_general(
        upstream, left_slab, (((2,), (2,)), ((0, 1), (0, 1))), preferred_element_type=jnp.float32
    )
    return (left_part.astype(jnp.bfloat16), right_part.astype(jnp.bfloat16))


def body(pair, proj_weights, cotangent):
    residues = pair.shape[1]
    local_rows = pair.shape[0]
    chans = pair.shape[2]
    ranks = lax.axis_size("rows")
    slab_width = chans // ranks
    normed_in, scale_in = layer_norm(pair.astype(jnp.float32), 2)
    normed_bf = normed_in.astype(jnp.bfloat16)
    edge_pre = jnp.einsum(
        "ikd,ndc->ncik", normed_bf, proj_weights[0:4], preferred_element_type=jnp.float32
    )
    gate_pre = jnp.einsum(
        "ikd,dc->ikc", normed_bf, proj_weights[4], preferred_element_type=jnp.float32
    )
    left_sig = jax.nn.sigmoid(edge_pre[1])
    right_sig = jax.nn.sigmoid(edge_pre[3])
    left_edge = (
        (left_sig * edge_pre[0])
        .astype(jnp.bfloat16)
        .reshape(ranks, slab_width, local_rows, residues)
    )
    right_edge = (
        (right_sig * edge_pre[2])
        .astype(jnp.bfloat16)
        .reshape(ranks, slab_width, local_rows, residues)
    )
    products, left_held, right_held = triangle_slab(
        (
            lax.all_to_all(left_edge, "rows", split_axis=0, concat_axis=2, tiled=True),
            lax.all_to_all(right_edge, "rows", split_axis=0, concat_axis=2, tiled=True),
        )
    )
    regrouped = lax.all_to_all(products, "rows", split_axis=2, concat_axis=0, tiled=True).reshape(
        chans, local_rows, residues
    )
    normed_mid, scale_mid = layer_norm(regrouped.astype(jnp.float32), 0)
    mid_bf = normed_mid.astype(jnp.bfloat16)
    projected = jnp.einsum(
        "cij,cd->ijd", mid_bf, proj_weights[5], preferred_element_type=jnp.float32
    )
    gating = jax.nn.sigmoid(gate_pre)
    update = (gating * projected).astype(jnp.bfloat16)
    upstream = cotangent.astype(jnp.float32)
    gated_up = (upstream * gating).astype(jnp.bfloat16)
    gate_grad = (upstream * projected * gating * (1.0 - gating)).astype(jnp.bfloat16)
    out_weights = jnp.stack(
        [
            jnp.einsum("ikd,ikc->dc", normed_bf, gate_grad, preferred_element_type=jnp.float32),
            jnp.einsum("cij,ijd->cd", mid_bf, gated_up, preferred_element_type=jnp.float32),
        ]
    )
    mid_grad = jnp.einsum(
        "ijd,cd->cij", gated_up, proj_weights[5], preferred_element_type=jnp.float32
    )
    prod_grad = norm_backward(normed_mid, scale_mid, mid_grad, 0).astype(jnp.bfloat16)
    prod_grad = prod_grad.reshape(ranks, slab_width, local_rows, residues)
    slab_grad = lax.all_to_all(prod_grad, "rows", split_axis=0, concat_axis=2, tiled=True)
    left_part, right_part = edge_backward(slab_grad, left_held, right_held)
    left_back, right_back = (
        lax.all_to_all(left_part, "rows", split_axis=2, concat_axis=0, tiled=True),
        lax.all_to_all(right_part, "rows", split_axis=2, concat_axis=0, tiled=True),
    )
    left_full = left_back.reshape(chans, local_rows, residues).astype(jnp.float32)
    right_full = right_back.reshape(chans, local_rows, residues).astype(jnp.float32)
    edge_grad = jnp.stack(
        [
            left_full * left_sig,
            left_full * edge_pre[0] * left_sig * (1.0 - left_sig),
            right_full * right_sig,
            right_full * edge_pre[2] * right_sig * (1.0 - right_sig),
        ]
    ).astype(jnp.bfloat16)
    in_weights = jnp.einsum(
        "ikd,ncik->ndc", normed_bf, edge_grad, preferred_element_type=jnp.float32
    )
    input_grad = jnp.einsum(
        "ncik,ndc->ikd", edge_grad, proj_weights[0:4], preferred_element_type=jnp.float32
    )
    input_grad = input_grad + jnp.einsum(
        "ikc,dc->ikd", gate_grad, proj_weights[4], preferred_element_type=jnp.float32
    )
    pair_grad = norm_backward(normed_in, scale_in, input_grad, 2).astype(jnp.bfloat16)
    totals = lax.psum(
        jnp.concatenate([in_weights, out_weights], axis=0).astype(jnp.bfloat16), "rows"
    ).astype(jnp.float32)
    weight_grads = totals / residues
    return (update, pair_grad, weight_grads)


def solution(mesh):
    in_specs = (P(("groups", "rows"), None, None), P(), P(("groups", "rows"), None, None))
    out_specs = (
        P(("groups", "rows"), None, None),
        P(("groups", "rows"), None, None),
        P("groups", None, None),
    )
    return jax.shard_map(body, mesh=mesh, in_specs=in_specs, out_specs=out_specs, check_vma=False)
```

profile of v0, /device:TPU:0, one launch (start us, length us, event | category | flops | bytes accessed | tf_op | source)
XLA Modules:
  0.0 318.2 jit_solution(738744233146156121)
XLA Ops:
  7.2 1.5 copy.69
  9.2 1.3 convolution_bitcast_fusion
  10.5 1.2 fusion.46
  11.7 2.0 copy-done
  13.7 1.1 copy.75
  14.8 7.4 %all-to-all-start.1 = ((bf16[16,8,16,256]{3,1,2,0:T(8,128)(2,1)}), bf16[16,8,16,256]{3,1,2,0:T(8,128)(2,1)S(1)}, u32[]{:S(2)}, u32[]{:S(2)}) async-start(bf16[16,8,16,256]{3,1,2,0:T(8,128)(2,1)} %copy.75), calls=%async_computation.1 | async-start | bytes 2097152 | tf_op jit(solution)/shard_map/all_to_all | solution.py:68
  22.2 1.1 copy.73
  23.3 21.9 %all-to-all-done.1 = bf16[16,8,16,256]{3,1,2,0:T(8,128)(2,1)S(1)} async-done(((bf16[16,8,16,256]{3,1,2,0:T(8,128)(2,1)}), bf16[16,8,16,256]{3,1,2,0:T(8,128)(2,1)S(1)}, u32[]{:S(2)}, u32[]{:S(2)}) %all-to-all-start.1) | async-done | bytes 1048608 | tf_op jit(solution)/shard_map/all_to_all | solution.py:68
  45.2 6.9 %all-to-all-start = ((bf16[16,8,16,256]{3,1,2,0:T(8,128)(2,1)}), bf16[16,8,16,256]{3,1,2,0:T(8,128)(2,1)}, u32[]{:S(2)}, u32[]{:S(2)}) async-start(bf16[16,8,16,256]{3,1,2,0:T(8,128)(2,1)} %copy.73), calls=%async_computation | async-start | bytes 2097152 | tf_op jit(solution)/shard_map/all_to_all | solution.py:67
  52.3 22.8 %all-to-all-done = bf16[16,8,16,256]{3,1,2,0:T(8,128)(2,1)} async-done(((bf16[16,8,16,256]{3,1,2,0:T(8,128)(2,1)}), bf16[16,8,16,256]{3,1,2,0:T(8,128)(2,1)}, u32[]{:S(2)}, u32[]{:S(2)}) %all-to-all-start) | async-done | bytes 1048608 | tf_op jit(solution)/shard_map/all_to_all | solution.py:67
  75.1 1.4 copy.74
  77.6 31.5 %all_to_all.72 = bf16[1,8,256,256]{3,1,0,2:T(8,128)(2,1)S(1)} all-to-all(bf16[1,8,256,256]{3,1,0,2:T(8,128)(2,1)S(1)} %copy.77), channel_id=1, replica_groups=mesh['groups'=2,'rows'=16] {'rows'}, dimensions={2} | all-to-all | bytes 2097152 | tf_op jit(solution)/shard_map/all_to_all | solution.py:71
  111.6 2.5 fusion.13
  114.1 1.6 bitcast_reduce_fusion
  115.8 1.6 fusion.47
  117.5 29.8 %all_to_all.73 = bf16[16,8,16,256]{3,1,2,0:T(8,128)(2,1)S(1)} all-to-all(bf16[16,8,16,256]{3,1,2,0:T(8,128)(2,1)S(1)} %copy.82), channel_id=1, replica_groups=mesh['groups'=2,'rows'=16] {'rows'}, dimensions={0} | all-to-all | bytes 2097152 | tf_op jit(solution)/shard_map/all_to_all | solution.py:95
  147.3 1.0 copy-done.4
  149.0 1.6 copy.84
  150.6 5.0 %all-to-all-start.4 = ((bf16[1,8,256,256]{3,1,0,2:T(8,128)(2,1)}), bf16[1,8,256,256]{3,1,0,2:T(8,128)(2,1)}, u32[]{:S(2)}, u32[]{:S(2)}) async-start(bf16[1,8,256,256]{3,1,0,2:T(8,128)(2,1)} %copy.84), calls=%async_computation.4 | async-start | bytes 2097152 | tf_op jit(solution)/shard_map/all_to_all | solution.py:98
  155.6 2.0 fusion.36
  157.7 1.6 copy.87
  159.3 19.3 %all-to-all-done.4 = bf16[1,8,256,256]{3,1,0,2:T(8,128)(2,1)} async-done(((bf16[1,8,256,256]{3,1,0,2:T(8,128)(2,1)}), bf16[1,8,256,256]{3,1,0,2:T(8,128)(2,1)}, u32[]{:S(2)}, u32[]{:S(2)}) %all-to-all-start.4) | async-done | bytes 1048608 | tf_op jit(solution)/shard_map/all_to_all | solution.py:98
  178.6 6.9 %all-to-all-start.5 = ((bf16[1,8,256,256]{3,1,0,2:T(8,128)(2,1)}), bf16[1,8,256,256]{3,1,0,2:T(8,128)(2,1)}, u32[]{:S(2)}, u32[]{:S(2)}) async-start(bf16[1,8,256,256]{3,1,0,2:T(8,128)(2,1)} %copy.87), calls=%async_computation.5 | async-start | bytes 2097152 | tf_op jit(solution)/shard_map/all_to_all | solution.py:99
  185.8 2.0 fusion.43
  187.8 2.9 fusion.42
  190.7 17.8 %all-to-all-done.5 = bf16[1,8,256,256]{3,1,0,2:T(8,128)(2,1)} async-done(((bf16[1,8,256,256]{3,1,0,2:T(8,128)(2,1)}), bf16[1,8,256,256]{3,1,0,2:T(8,128)(2,1)}, u32[]{:S(2)}, u32[]{:S(2)}) %all-to-all-start.5) | async-done | bytes 1048608 | tf_op jit(solution)/shard_map/all_to_all | solution.py:99
  208.5 5.0 %fusion.24 = (bf16[1,128,16,256]{3,1,0,2:T(8,128)(2,1)S(1)}, bf16[1,128,16,256]{3,1,0,2:T(8,128)(2,1)S(1)}, bf16[1,128,16,256]{3,1,0,2:T(8,128)(2,1)S(1)}, bf16[1,128,16,256]{3,1,0,2:T(8,128)(2,1)S(1)}) fusion(f32[4,128,16,256]{3,1,0,2:T(8,128)} %copy-done, bf16[1,8,16,16,256]{4,1,3,2,0:T(8,128)(2,1)} %bitcast.53, bf16[1,8,16,16,256]{4,1,3,2,0:T(8,128)(2,1)} %bitcast.51), kind=kLoop, calls=%fused_computation.37 | loop fusion | flops 11534336 | bytes 14680064 | tf_op jit(solution)/shard_map/convert.17
  213.5 1.3 fusion.39
  217.5 1.6 fusion.8
  219.1 2.3 copy.93
  221.3 88.2 %all-reduce.2.cloned.1.call-done = bf16[6,128,128]{1,2,0:T(8,128)(2,1)} async-done(((bf16[6,128,128]{1,2,0:T(8,128)(2,1)}), bf16[6,128,128]{1,2,0:T(8,128)(2,1)}) %all-reduce.2.cloned.1.call-update) | async-done | bytes 196624 | tf_op jit(solution)/shard_map/psum | solution.py:121
  309.5 1.0 convert_multiply_fusion.2
  (45 shorter events, 8.8 us)
Async XLA Ops:
  7.2 2.1 copy-start.9
  10.5 3.2 %copy-start = (f32[4,128,16,256]{3,1,0,2:T(8,128)}, f32[4,128,16,256]{3,1,0,2:T(8,128)S(1)}, u32[]{:S(2)}) copy-start(f32[4,128,16,256]{3,1,0,2:T(8,128)S(1)} %convolution_bitcast_fusion) | copy-start | bytes 25165828
  14.8 30.3 %all-to-all-start.1 = ((bf16[16,8,16,256]{3,1,2,0:T(8,128)(2,1)}), bf16[16,8,16,256]{3,1,2,0:T(8,128)(2,1)S(1)}, u32[]{:S(2)}, u32[]{:S(2)}) async-start(bf16[16,8,16,256]{3,1,2,0:T(8,128)(2,1)} %copy.75), calls=%async_computation.1 | async-start | bytes 2097152 | tf_op jit(solution)/shard_map/all_to_all | solution.py:68
  45.2 29.9 %all-to-all-start = ((bf16[16,8,16,256]{3,1,2,0:T(8,128)(2,1)}), bf16[16,8,16,256]{3,1,2,0:T(8,128)(2,1)}, u32[]{:S(2)}, u32[]{:S(2)}) async-start(bf16[16,8,16,256]{3,1,2,0:T(8,128)(2,1)} %copy.73), calls=%async_computation | async-start | bytes 2097152 | tf_op jit(solution)/shard_map/all_to_all | solution.py:67
  52.3 24.7 %copy-start.2 = (bf16[1,8,16,16,256]{4,3,2,1,0:T(8,128)(2,1)}, bf16[1,8,16,16,256]{4,3,2,1,0:T(8,128)(2,1)S(1)}, u32[]{:S(2)}) copy-start(bf16[1,8,16,16,256]{4,3,2,1,0:T(8,128)(2,1)S(1)} %copy.76) | copy-start | bytes 3145732
  76.5 1.1 copy-start.1
  110.4 1.2 copy-start.7
  114.1 1.6 copy-start.5
  117.5 31.0 %copy-start.3 = (bf16[1,8,16,16,256]{4,3,2,1,0:T(8,128)(2,1)S(1)}, bf16[1,8,16,16,256]{4,3,2,1,0:T(8,128)(2,1)}, u32[]{:S(2)}) copy-start(bf16[1,8,16,16,256]{4,3,2,1,0:T(8,128)(2,1)} %copy-done.2) | copy-start | bytes 3145732
  147.3 1.0 copy-start.4
  150.6 28.0 %all-to-all-start.4 = ((bf16[1,8,256,256]{3,1,0,2:T(8,128)(2,1)}), bf16[1,8,256,256]{3,1,0,2:T(8,128)(2,1)}, u32[]{:S(2)}, u32[]{:S(2)}) async-start(bf16[1,8,256,256]{3,1,0,2:T(8,128)(2,1)} %copy.84), calls=%async_computation.4 | async-start | bytes 2097152 | tf_op jit(solution)/shard_map/all_to_all | solution.py:98
  178.6 29.9 %all-to-all-start.5 = ((bf16[1,8,256,256]{3,1,0,2:T(8,128)(2,1)}), bf16[1,8,256,256]{3,1,0,2:T(8,128)(2,1)}, u32[]{:S(2)}, u32[]{:S(2)}) async-start(bf16[1,8,256,256]{3,1,0,2:T(8,128)(2,1)} %copy.87), calls=%async_computation.5 | async-start | bytes 2097152 | tf_op jit(solution)/shard_map/all_to_all | solution.py:99
  185.5 124.0 %all-reduce.2.cloned.1.call-start = ((), (), s32[]{:S(2)}) async-start(), calls=%async_computation.6 | async-start | bytes 393216 | tf_op jit(solution)/shard_map/psum | solution.py:121
  185.8 2.0 copy-start.6
  214.8 1.2 copy-start.8
Sparse Core Ops, SparseCore 0:
  217.6 91.8 all-reduce.1
where the time goes:
time: 319 us; the launch traced here: 318 us
  waiting for transfers between devices  170 us (53%)
  blocking collectives  61.3 us (19%)
  starting transfers between devices  26.5 us (8%)
  local copies, waits for them, and re-layouts  16.9 us (5%)
  matrix products  16.5 us (5%)
  between operations  14.4 us (5%)
  other arithmetic  12.6 us (4%)
    psum x1, waiting for transfers between devices, body(): lax.psum(jnp.concatenate([in_weights, out_weights], axis=0).astype(jnp.bf...  88.2 us
    all_to_all x1, blocking collectives, body(): lax.all_to_all(products, 'rows', split_axis=2, concat_axis=0, tiled=True)  31.5 us
    all_to_all x1, blocking collectives, body(): lax.all_to_all(prod_grad, 'rows', split_axis=0, concat_axis=2, tiled=True)  29.8 us
    all_to_all x1, waiting for transfers between devices, body(): lax.all_to_all(left_edge, 'rows', split_axis=0, concat_axis=2, tiled=True)  22.8 us
    all_to_all x1, waiting for transfers between devices, body(): lax.all_to_all(right_edge, 'rows', split_axis=0, concat_axis=2, tiled=True)  21.9 us
    all_to_all x1, waiting for transfers between devices, body(): lax.all_to_all(left_part, 'rows', split_axis=2, concat_axis=0, tiled=True)  19.3 us
    all_to_all x1, waiting for transfers between devices, body(): lax.all_to_all(right_part, 'rows', split_axis=2, concat_axis=0, tiled=True)  17.8 us
    unnamed x23, local copies, waits for them, and re-layouts  8.91 us
  transfers between devices with their start and end apart: 5, of which 5 were waited for; matrix products, arithmetic and copies ran while one was open for 4% of the time, Pallas kernels for 0%

commit v1 on v0

--- a/solution.py
+++ b/solution.py
@@ -2,6 +2,11 @@
 import jax.numpy as jnp
 from jax import lax
 from jax.sharding import PartitionSpec as P
+
+
+def gather_and_add(shard, name):
+    pieces = lax.all_gather(shard, name)
+    return jnp.sum(pieces, axis=0)
 
 
 def layer_norm(values, along_dim):
@@ -118,7 +123,7 @@
         "ikc,dc->ikd", gate_grad, proj_weights[4], preferred_element_type=jnp.float32
     )
     pair_grad = norm_backward(normed_in, scale_in, input_grad, 2).astype(jnp.bfloat16)
-    totals = lax.psum(
+    totals = gather_and_add(
         jnp.concatenate([in_weights, out_weights], axis=0).astype(jnp.bfloat16), "rows"
     ).astype(jnp.float32)
     weight_grads = totals / residues

time: 319 us -> 274 us (0.86)
  waiting for transfers between devices: 170 us -> 123 us
    psum x1 -> x0, waiting for transfers between devices: 88.2 us -> none  [body(): lax.psum(jnp.concatenate([in_weights, out_weights], axis=0).astype(jnp.bf...]
    all_gather x0 -> x1, waiting for transfers between devices: none -> 42.4 us  [gather_and_add(): pieces = lax.all_gather(shard, name)]
    unnamed x23 -> x36, local copies, waits for them, and re-layouts: 8.91 us -> 7.73 us
  transfers between devices with their start and end apart: 5 -> 5, of which waited for: 5 -> 5; matrix products, arithmetic and copies ran while one was open for 4% -> 6% of each run, Pallas kernels for 0% -> 0%
where the time goes in v1:
time: 274 us
  waiting for transfers between devices  123 us (45%)
  blocking collectives  61.3 us (22%)
  starting transfers between devices  26.5 us (10%)
  matrix products  19.2 us (7%)
  local copies, waits for them, and re-layouts  16.5 us (6%)
  between operations  14.5 us (5%)
  other arithmetic  12.6 us (5%)
    all_gather x1, waiting for transfers between devices, gather_and_add(): pieces = lax.all_gather(shard, name)  42.4 us
    all_to_all x1, blocking collectives, body(): lax.all_to_all(products, 'rows', split_axis=2, concat_axis=0, tiled=True)  31.5 us
    all_to_all x1, blocking collectives, body(): lax.all_to_all(prod_grad, 'rows', split_axis=0, concat_axis=2, tiled=True)  29.8 us
    all_to_all x1, waiting for transfers between devices, body(): lax.all_to_all(left_edge, 'rows', split_axis=0, concat_axis=2, tiled=True)  22.8 us
    all_to_all x1, waiting for transfers between devices, body(): lax.all_to_all(right_edge, 'rows', split_axis=0, concat_axis=2, tiled=True)  21.9 us
    all_to_all x1, waiting for transfers between devices, body(): lax.all_to_all(left_part, 'rows', split_axis=2, concat_axis=0, tiled=True)  19.3 us
    all_to_all x1, waiting for transfers between devices, body(): lax.all_to_all(right_part, 'rows', split_axis=2, concat_axis=0, tiled=True)  16.6 us
    unnamed x36, local copies, waits for them, and re-layouts  7.73 us
  transfers between devices with their start and end apart: 5, of which 5 were waited for; matrix products, arithmetic and copies ran while one was open for 6% of the time, Pallas kernels for 0%

profile of v1, /device:TPU:0, one launch (start us, length us, event | category | flops | bytes accessed | tf_op | source)
XLA Modules:
  0.0 273.8 jit_solution(4895416975351418070)
XLA Ops:
  7.2 1.5 copy.69
  9.2 1.3 convolution_bitcast_fusion
  10.5 1.2 fusion.46
  11.7 2.0 copy-done
  13.8 1.1 copy.75
  14.9 7.4 %all-to-all-start.1 = ((bf16[16,8,16,256]{3,1,2,0:T(8,128)(2,1)}), bf16[16,8,16,256]{3,1,2,0:T(8,128)(2,1)S(1)}, u32[]{:S(2)}, u32[]{:S(2)}) async-start(bf16[16,8,16,256]{3,1,2,0:T(8,128)(2,1)} %copy.75), calls=%async_computation.1 | async-start | bytes 2097152 | tf_op jit(solution)/shard_map/all_to_all | solution.py:73
  22.2 1.1 copy.73
  23.3 21.9 %all-to-all-done.1 = bf16[16,8,16,256]{3,1,2,0:T(8,128)(2,1)S(1)} async-done(((bf16[16,8,16,256]{3,1,2,0:T(8,128)(2,1)}), bf16[16,8,16,256]{3,1,2,0:T(8,128)(2,1)S(1)}, u32[]{:S(2)}, u32[]{:S(2)}) %all-to-all-start.1) | async-done | bytes 1048608 | tf_op jit(solution)/shard_map/all_to_all | solution.py:73
  45.2 6.9 %all-to-all-start = ((bf16[16,8,16,256]{3,1,2,0:T(8,128)(2,1)}), bf16[16,8,16,256]{3,1,2,0:T(8,128)(2,1)}, u32[]{:S(2)}, u32[]{:S(2)}) async-start(bf16[16,8,16,256]{3,1,2,0:T(8,128)(2,1)} %copy.73), calls=%async_computation | async-start | bytes 2097152 | tf_op jit(solution)/shard_map/all_to_all | solution.py:72
  52.3 22.8 %all-to-all-done = bf16[16,8,16,256]{3,1,2,0:T(8,128)(2,1)} async-done(((bf16[16,8,16,256]{3,1,2,0:T(8,128)(2,1)}), bf16[16,8,16,256]{3,1,2,0:T(8,128)(2,1)}, u32[]{:S(2)}, u32[]{:S(2)}) %all-to-all-start) | async-done | bytes 1048608 | tf_op jit(solution)/shard_map/all_to_all | solution.py:72
  75.1 1.4 copy.74
  77.6 31.5 %all_to_all.72 = bf16[1,8,256,256]{3,1,0,2:T(8,128)(2,1)S(1)} all-to-all(bf16[1,8,256,256]{3,1,0,2:T(8,128)(2,1)S(1)} %copy.77), channel_id=1, replica_groups=mesh['groups'=2,'rows'=16] {'rows'}, dimensions={2} | all-to-all | bytes 2097152 | tf_op jit(solution)/shard_map/all_to_all | solution.py:76
  111.6 2.5 fusion.13
  114.2 1.6 bitcast_reduce_fusion
  115.8 1.6 fusion.47
  117.6 29.8 %all_to_all.73 = bf16[16,8,16,256]{3,1,2,0:T(8,128)(2,1)S(1)} all-to-all(bf16[16,8,16,256]{3,1,2,0:T(8,128)(2,1)S(1)} %copy.82), channel_id=1, replica_groups=mesh['groups'=2,'rows'=16] {'rows'}, dimensions={0} | all-to-all | bytes 2097152 | tf_op jit(solution)/shard_map/all_to_all | solution.py:100
  147.3 1.0 copy-done.4
  149.0 1.6 copy.84
  150.6 5.0 %all-to-all-start.4 = ((bf16[1,8,256,256]{3,1,0,2:T(8,128)(2,1)}), bf16[1,8,256,256]{3,1,0,2:T(8,128)(2,1)}, u32[]{:S(2)}, u32[]{:S(2)}) async-start(bf16[1,8,256,256]{3,1,0,2:T(8,128)(2,1)} %copy.84), calls=%async_computation.4 | async-start | bytes 2097152 | tf_op jit(solution)/shard_map/all_to_all | solution.py:103
  155.7 2.0 fusion.36
  157.7 1.6 copy.87
  159.3 19.3 %all-to-all-done.4 = bf16[1,8,256,256]{3,1,0,2:T(8,128)(2,1)} async-done(((bf16[1,8,256,256]{3,1,0,2:T(8,128)(2,1)}), bf16[1,8,256,256]{3,1,0,2:T(8,128)(2,1)}, u32[]{:S(2)}, u32[]{:S(2)}) %all-to-all-start.4) | async-done | bytes 1048608 | tf_op jit(solution)/shard_map/all_to_all | solution.py:103
  178.7 6.9 %all-to-all-start.5 = ((bf16[1,8,256,256]{3,1,0,2:T(8,128)(2,1)}), bf16[1,8,256,256]{3,1,0,2:T(8,128)(2,1)}, u32[]{:S(2)}, u32[]{:S(2)}) async-start(bf16[1,8,256,256]{3,1,0,2:T(8,128)(2,1)} %copy.87), calls=%async_computation.5 | async-start | bytes 2097152 | tf_op jit(solution)/shard_map/all_to_all | solution.py:104
  185.9 2.6 fusion.43
  188.4 3.5 %fusion.42 = bf16[1,1,128,128]{2,3,1,0:T(8,128)(2,1)} fusion(f32[16,1,8,16,256]{4,3,0,2,1:T(8,128)S(1)} %get-tuple-element.29, f32[16,256]{1,0:T(8,128)S(1)} %add_rsqrt_fusion, f32[16,256]{1,0:T(8,128)S(1)} %broadcast_multiply_fusion.4, f32[16,256,128]{2,1,0:T(8,128)S(1)} %copy-done.6, bf16[16,256,128]{2,1,0:T(8,128)(2,1)} %param.5), kind=kOutput, calls=%fused_computation.72 | convolution fusion | flops 137379840 | bytes 5308416 | tf_op jit(solution)/shard_map/cij,ijd->cd/dot_general | solution.py:92
  192.0 16.6 %all-to-all-done.5 = bf16[1,8,256,256]{3,1,0,2:T(8,128)(2,1)} async-done(((bf16[1,8,256,256]{3,1,0,2:T(8,128)(2,1)}), bf16[1,8,256,256]{3,1,0,2:T(8,128)(2,1)}, u32[]{:S(2)}, u32[]{:S(2)}) %all-to-all-start.5) | async-done | bytes 1048608 | tf_op jit(solution)/shard_map/all_to_all | solution.py:104
  208.6 4.9 %fusion.24 = (bf16[1,128,16,256]{3,1,0,2:T(8,128)(2,1)S(1)}, bf16[1,128,16,256]{3,1,0,2:T(8,128)(2,1)S(1)}, bf16[1,128,16,256]{3,1,0,2:T(8,128)(2,1)S(1)}, bf16[1,128,16,256]{3,1,0,2:T(8,128)(2,1)S(1)}) fusion(f32[4,128,16,256]{3,1,0,2:T(8,128)} %copy-done, bf16[1,8,16,16,256]{4,1,3,2,0:T(8,128)(2,1)} %bitcast.54, bf16[1,8,16,16,256]{4,1,3,2,0:T(8,128)(2,1)} %bitcast.52), kind=kLoop, calls=%fused_computation.37 | loop fusion | flops 11534336 | bytes 14680064 | tf_op jit(solution)/shard_map/convert.19
  213.5 1.3 fusion.39
  215.8 2.2 fusion.55
  219.5 1.3 copy.95
  220.8 42.4 %all-gather.2.cloned.1.call-done = bf16[16,6,128,128]{3,2,1,0:T(8,128)(2,1)} async-done(((bf16[1,6,128,128]{3,2,1,0:T(8,128)(2,1)}), bf16[16,6,128,128]{3,2,1,0:T(8,128)(2,1)}) %all-gather.2.cloned.1.call-update) | async-done | bytes 3145744 | tf_op jit(solution)/shard_map/all_gather | solution.py:8
  263.3 2.5 reduce_sum.92
  (60 shorter events, 8.7 us)
Async XLA Ops:
  7.2 2.1 copy-start.11
  9.2 204.3 %copy-start.12 = (f32[16,256]{1,0:T(8,128)}, f32[16,256]{1,0:T(8,128)S(1)}, u32[]{:S(2)}) copy-start(f32[16,256]{1,0:T(8,128)S(1)} %add_rsqrt_fusion.1) | copy-start | bytes 49156
  10.5 3.2 %copy-start = (f32[4,128,16,256]{3,1,0,2:T(8,128)}, f32[4,128,16,256]{3,1,0,2:T(8,128)S(1)}, u32[]{:S(2)}) copy-start(f32[4,128,16,256]{3,1,0,2:T(8,128)S(1)} %convolution_bitcast_fusion) | copy-start | bytes 25165828
  14.9 30.3 %all-to-all-start.1 = ((bf16[16,8,16,256]{3,1,2,0:T(8,128)(2,1)}), bf16[16,8,16,256]{3,1,2,0:T(8,128)(2,1)S(1)}, u32[]{:S(2)}, u32[]{:S(2)}) async-start(bf16[16,8,16,256]{3,1,2,0:T(8,128)(2,1)} %copy.75), calls=%async_computation.1 | async-start | bytes 2097152 | tf_op jit(solution)/shard_map/all_to_all | solution.py:73
  45.2 29.9 %all-to-all-start = ((bf16[16,8,16,256]{3,1,2,0:T(8,128)(2,1)}), bf16[16,8,16,256]{3,1,2,0:T(8,128)(2,1)}, u32[]{:S(2)}, u32[]{:S(2)}) async-start(bf16[16,8,16,256]{3,1,2,0:T(8,128)(2,1)} %copy.73), calls=%async_computation | async-start | bytes 2097152 | tf_op jit(solution)/shard_map/all_to_all | solution.py:72
  52.3 24.7 %copy-start.2 = (bf16[1,8,16,16,256]{4,3,2,1,0:T(8,128)(2,1)}, bf16[1,8,16,16,256]{4,3,2,1,0:T(8,128)(2,1)S(1)}, u32[]{:S(2)}) copy-start(bf16[1,8,16,16,256]{4,3,2,1,0:T(8,128)(2,1)S(1)} %copy.76) | copy-start | bytes 3145732
  76.5 1.1 copy-start.1
  110.4 1.2 copy-start.7
  114.2 1.6 copy-start.5
  117.6 31.0 %copy-start.3 = (bf16[1,8,16,16,256]{4,3,2,1,0:T(8,128)(2,1)S(1)}, bf16[1,8,16,16,256]{4,3,2,1,0:T(8,128)(2,1)}, u32[]{:S(2)}) copy-start(bf16[1,8,16,16,256]{4,3,2,1,0:T(8,128)(2,1)} %copy-done.2) | copy-start | bytes 3145732
  147.3 1.0 copy-start.4
  150.6 28.0 %all-to-all-start.4 = ((bf16[1,8,256,256]{3,1,0,2:T(8,128)(2,1)}), bf16[1,8,256,256]{3,1,0,2:T(8,128)(2,1)}, u32[]{:S(2)}, u32[]{:S(2)}) async-start(bf16[1,8,256,256]{3,1,0,2:T(8,128)(2,1)} %copy.84), calls=%async_computation.4 | async-start | bytes 2097152 | tf_op jit(solution)/shard_map/all_to_all | solution.py:103
  178.7 29.9 %all-to-all-start.5 = ((bf16[1,8,256,256]{3,1,0,2:T(8,128)(2,1)}), bf16[1,8,256,256]{3,1,0,2:T(8,128)(2,1)}, u32[]{:S(2)}, u32[]{:S(2)}) async-start(bf16[1,8,256,256]{3,1,0,2:T(8,128)(2,1)} %copy.87), calls=%async_computation.5 | async-start | bytes 2097152 | tf_op jit(solution)/shard_map/all_to_all | solution.py:104
  185.6 77.7 %all-gather.2.cloned.1.call-start = ((), (), s32[]{:S(2)}) async-start(), calls=%async_computation.6 | async-start | bytes 3342336 | tf_op jit(solution)/shard_map/all_gather | solution.py:8
  185.9 2.6 copy-start.6
  213.5 1.3 copy-start.8
  213.5 1.3 copy-start.9
  213.5 1.3 copy-start.14
  213.5 1.3 copy-start.15
  215.8 2.3 copy-start.10
  215.8 2.3 copy-start.13
Sparse Core Ops, SparseCore 0:
  215.9 47.3 all-gather.1
